TPU v7x, 32 devices: a whole 2x2x4 slice. The times are simulated.
32 devices in a mesh: tm: 8 (over z, x), head: 4 (over y, core).
Axes of the slice: x: 2, y: 2, z: 4, core: 2. Of those that a mesh axis runs over, the one named last changes fastest.
Arguments:
- video_q: bfloat16 [1024, 3072], P('tm', 'head'), may hold values from -12 to 12
- video_k: bfloat16 [1024, 3072], P('tm', 'head'), may hold values from -9 to 9
- video_v: bfloat16 [1024, 3072], P('tm', 'head'), may hold values from -6 to 6
- captions: bfloat16 [2048, 4096], P(('tm', 'head')), may hold values from -12 to 12
- text_k_weight: bfloat16 [4096, 3072], P(None, 'head'), may hold values from -0.09375 to 0.09375
- text_v_weight: bfloat16 [4096, 3072], P(None, 'head'), may hold values from -0.09375 to 0.09375
- shot_spans: int32 [8, 2], replicated, may hold values from 0 to 1024, as said below
- caption_lens: int32 [8], replicated, may hold values from 1 to 256, 1280 in all
Outputs:
- attended: bfloat16 [1024, 3072], P('tm', 'head')
Inputs may be any that keep to these rules, and one draw needn't show every extreme that they name: Shot s holds tokens shot_spans[s, 0] to shot_spans[s, 1] - 1; the shots follow one another without gaps, the first starts at 0, the last ends at 1024, each holds one token or more. Caption slots c < caption_lens[s] of shot s are live.
All inputs are finite; a program needn't handle non-finite values.
Results may differ from a plain program's by a relative error of at most 0.0077.
Values may be sent and summed in bfloat16 or wider, within the bound.
A program may use at most 192 MiB of HBM per device.

v0:
```python
import math

import jax
import jax.numpy as jnp
from jax import lax
from jax.sharding import PartitionSpec as P

HD = 128
SHOTS = 8


def per_device(
    video_q, video_k, video_v, captions, text_k_weight, text_v_weight, shot_spans, caption_lens
):
    tok_rows = video_q.shape[0]
    queries = video_q.reshape(tok_rows, -1, HD)
    heads_here = queries.shape[1]
    inv_scale = 1.0 / math.sqrt(HD)
    offset_tok = lax.axis_index("tm") * tok_rows
    position = offset_tok + jnp.arange(tok_rows, dtype=jnp.int32)
    shot_ids = jnp.arange(SHOTS, dtype=jnp.int32)
    inside = (position[:, None] >= shot_spans[None, :, 0]) & (
        position[:, None] < shot_spans[None, :, 1]
    )
    shot_of = jnp.sum(jnp.where(inside, shot_ids[None, :], 0), axis=1)

    def absorb(running, key_rows, value_rows, allowed):
        run_max, run_sum, run_num = running
        key_heads = key_rows.reshape(key_rows.shape[0], -1, HD)
        value_heads = value_rows.reshape(value_rows.shape[0], -1, HD)
        scores = (
            jnp.einsum("thd,nhd->thn", queries, key_heads, preferred_element_type=jnp.float32)
            * inv_scale
        )
        if allowed is not None:
            scores = jnp.where(allowed[:, None, :], scores, -jnp.inf)
        new_max = jnp.maximum(run_max, jnp.max(scores, axis=2))
        safe_max = jnp.where(new_max == -jnp.inf, 0.0, new_max)
        rescale = jnp.exp(run_max - safe_max)
        weights = jnp.exp(scores - safe_max[:, :, None])
        run_sum = run_sum * rescale + jnp.sum(weights, axis=2)
        run_num = run_num * rescale[:, :, None] + jnp.einsum(
            "thn,nhd->thd",
            weights.astype(jnp.bfloat16),
            value_heads,
            preferred_element_type=jnp.float32,
        )
        return (new_max, run_sum, run_num)

    running = (
        jnp.full((tok_rows, heads_here), -jnp.inf, jnp.float32),
        jnp.zeros((tok_rows, heads_here), jnp.float32),
        jnp.zeros((tok_rows, heads_here, HD), jnp.float32),
    )
    gathered_keys, gathered_values = (
        lax.all_gather(video_k, "tm", axis=0, tiled=True),
        lax.all_gather(video_v, "tm", axis=0, tiled=True),
    )
    running = absorb(running, gathered_keys, gathered_values, None)
    caption_block = lax.all_gather(captions, "head", axis=0, tiled=True)
    text_keys = jnp.dot(caption_block, text_k_weight, preferred_element_type=jnp.float32).astype(
        jnp.bfloat16
    )
    text_values = jnp.dot(caption_block, text_v_weight, preferred_element_type=jnp.float32).astype(
        jnp.bfloat16
    )
    every_key = lax.all_gather(text_keys, "tm", axis=0, tiled=True)
    every_value = lax.all_gather(text_values, "tm", axis=0, tiled=True)
    row_index = jnp.arange(every_key.shape[0], dtype=jnp.int32)
    row_shot = row_index % SHOTS
    row_pos = row_index // SHOTS
    row_len = jnp.sum(
        jnp.where(row_shot[:, None] == shot_ids[None, :], caption_lens[None, :], 0), axis=1
    )
    running = absorb(
        running,
        every_key,
        every_value,
        (shot_of[:, None] == row_shot[None, :]) & (row_pos < row_len)[None, :],
    )
    run_max, run_sum, run_num = running
    return (run_num / run_sum[:, :, None]).astype(jnp.bfloat16).reshape(tok_rows, -1)


def solution(mesh):
    placed = (
        P("tm", "head"),
        P("tm", "head"),
        P("tm", "head"),
        P(("tm", "head"), None),
        P(None, "head"),
        P(None, "head"),
        P(),
        P(),
    )
    return jax.shard_map(
        per_device, mesh=mesh, in_specs=placed, out_specs=P("tm", "head"), check_vma=False
    )
```

profile of v0, /device:TPU:0, one launch (start us, length us, event | category | flops | bytes accessed | tf_op | source)
XLA Modules:
  0.0 268.8 jit_solution(14224737221335362114)
XLA Ops:
  6.5 0.0 all-gather.10.cloned.1.call-start
  6.5 0.7 all-gather.10.cloned.1.call-update
  7.3 0.0 all-gather.8.cloned.1.call-start
  7.3 0.7 all-gather.8.cloned.1.call-update
  8.0 0.0 all-gather.6.cloned.1.call-start
  8.1 1.8 copy.29
  9.8 0.0 all-gather.6.cloned.1.call-update
  9.8 0.0 all-gather.12.cloned.1.call-start
  9.9 24.4 %all-gather.10.cloned.1.call-done = bf16[256,4096]{1,0:T(8,128)(2,1)} async-done(((bf16[64,4096]{1,0:T(8,128)(2,1)}), bf16[256,4096]{1,0:T(8,128)(2,1)}) %all-gather.10.cloned.1.call-update) | async-done | bytes 2097168 | tf_op jit(solution)/shard_map/all_gather | solution.py:60
  34.2 0.0 copy-start.5
  34.2 6.1 %convolution_convert_fusion.1 = bf16[256,768]{1,0:T(8,128)(2,1)} fusion(bf16[256,4096]{1,0:T(8,128)(2,1)} %all-gather.10.cloned.1.call-done, bf16[4096,768]{1,0:T(8,128)(2,1)} %param.12), kind=kOutput, calls=%fused_computation.19 | convolution fusion | flops 1610809344 | bytes 8781824 | tf_op jit(solution)/shard_map/dot_general | solution.py:61
  40.4 0.0 all-gather.12.cloned.1.call-update
  40.4 0.0 copy-start.2
  40.4 0.0 copy-start.4
  40.4 0.0 copy-start.3
  40.4 0.0 all-gather.14.cloned.1.call-start
  40.5 0.0 copy-done.5
  40.5 5.4 %convolution_convert_fusion = bf16[256,768]{1,0:T(8,128)(2,1)} fusion(bf16[256,4096]{1,0:T(8,128)(2,1)S(1)} %copy-done.5, bf16[4096,768]{1,0:T(8,128)(2,1)} %param.13), kind=kOutput, calls=%fused_computation.18 | convolution fusion | flops 1610809344 | bytes 8781824 | tf_op jit(solution)/shard_map/dot_general | solution.py:64
  45.9 0.0 all-gather.14.cloned.1.call-update
  45.9 0.0 copy-done.2
  45.9 0.8 copy.30
  46.7 0.0 copy-done.4
  46.7 0.1 select_reduce_fusion
  46.8 0.0 copy-done.3
  46.9 0.1 select_reduce_fusion.1
  47.0 1.5 compare_and_fusion
  48.4 32.2 %all-gather.8.cloned.1.call-done = bf16[1024,768]{1,0:T(8,128)(2,1)} async-done(((bf16[128,768]{1,0:T(8,128)(2,1)}), bf16[1024,768]{1,0:T(8,128)(2,1)}) %all-gather.8.cloned.1.call-update) | async-done | bytes 1572880 | tf_op jit(solution)/shard_map/all_gather | solution.py:57
  80.6 2.6 copy.33
  83.2 43.6 %all-gather.6.cloned.1.call-done = bf16[1024,768]{0,1:T(8,128)(2,1)} async-done(((bf16[128,768]{0,1:T(8,128)(2,1)}), bf16[1024,768]{0,1:T(8,128)(2,1)}) %all-gather.6.cloned.1.call-update) | async-done | bytes 1572880 | tf_op jit(solution)/shard_map/all_gather | solution.py:56
  126.8 2.1 bitcast_reduce_fusion
  128.9 58.6 %all-gather.12.cloned.1.call-done = bf16[2048,768]{1,0:T(8,128)(2,1)} async-done(((bf16[256,768]{1,0:T(8,128)(2,1)}), bf16[2048,768]{1,0:T(8,128)(2,1)}) %all-gather.12.cloned.1.call-update) | async-done | bytes 3145744 | tf_op jit(solution)/shard_map/all_gather | solution.py:67
  187.5 4.7 %copy.35 = bf16[2048,768]{0,1:T(8,128)(2,1)} copy(bf16[2048,768]{1,0:T(8,128)(2,1)} %all-gather.12.cloned.1.call-done) | data formatting | bytes 6291456 | tf_op jit(solution)/shard_map/all_gather | solution.py:67
  192.3 3.6 %fusion.2 = (f32[128,6]{0,1:T(8,128)S(1)}, f32[6,2048,128]{2,1,0:T(8,128)S(1)}) fusion(pred[128,2048]{0,1:T(8,128)(4,1)S(1)} %compare_and_fusion, bf16[2048,6,128]{0,2,1:T(8,128)(2,1)} %bitcast.67, bf16[128,6,128]{0,2,1:T(8,128)(2,1)} %bitcast.70), kind=kOutput, calls=%fused_computation.4 | convolution fusion | flops 407371008 | bytes 9899008 | tf_op jit(solution)/shard_map/thd,nhd->thn/dot_general | solution.py:32
  195.9 0.0 copy-start
  195.9 2.6 copy-done
  198.5 1.3 fusion
  199.9 48.8 %all-gather.14.cloned.1.call-done = bf16[2048,768]{1,0:T(8,128)(2,1)} async-done(((bf16[256,768]{1,0:T(8,128)(2,1)}), bf16[2048,768]{1,0:T(8,128)(2,1)}) %all-gather.14.cloned.1.call-update) | async-done | bytes 3145744 | tf_op jit(solution)/shard_map/all_gather | solution.py:68
  248.7 4.7 %copy.38 = bf16[2048,768]{0,1:T(8,128)(2,1)} copy(bf16[2048,768]{1,0:T(8,128)(2,1)} %all-gather.14.cloned.1.call-done) | data formatting | bytes 6291456 | tf_op jit(solution)/shard_map/all_gather | solution.py:68
  253.4 5.6 %fusion.28 = f32[128,6,128]{0,2,1:T(8,128)S(1)} fusion(bf16[2048,6,128]{0,2,1:T(8,128)(2,1)} %bitcast.68, f32[6,2048,128]{2,1,0:T(8,128)} %copy-done, f32[128,6]{0,1:T(8,128)S(1)} %get-tuple-element.8, pred[128,2048]{0,1:T(8,128)(4,1)S(1)} %compare_and_fusion), kind=kOutput, calls=%fused_computation.24 | convolution fusion | flops 408944640 | bytes 10095616 | tf_op jit(solution)/shard_map/thn,nhd->thd/dot_general | solution.py:42
  259.0 0.0 copy-start.1
  259.0 0.5 fusion.10
  259.6 0.8 copy-done.1
  260.4 1.0 fusion.34
  261.4 0.8 copy.40
  (6 shorter events, 0.0 us)
Async XLA Ops:
  6.5 27.7 %all-gather.10.cloned.1.call-start = ((), (), s32[]{:S(2)}) async-start(), calls=%async_computation.2 | async-start | bytes 2621440 | tf_op jit(solution)/shard_map/all_gather | solution.py:60
  7.3 73.4 %all-gather.8.cloned.1.call-start = ((), (), s32[]{:S(2)}) async-start(), calls=%async_computation.1 | async-start | bytes 1769472 | tf_op jit(solution)/shard_map/all_gather | solution.py:57
  8.0 118.8 %all-gather.6.cloned.1.call-start = ((), (), s32[]{:S(2)}) async-start(), calls=%async_computation | async-start | bytes 1769472 | tf_op jit(solution)/shard_map/all_gather | solution.py:56
  9.8 177.7 %all-gather.12.cloned.1.call-start = ((), (), s32[]{:S(2)}) async-start(), calls=%async_computation.3 | async-start | bytes 3538944 | tf_op jit(solution)/shard_map/all_gather | solution.py:67
  34.2 6.2 %copy-start.5 = (bf16[256,4096]{1,0:T(8,128)(2,1)S(1)}, bf16[256,4096]{1,0:T(8,128)(2,1)}, u32[]{:S(2)}) copy-start(bf16[256,4096]{1,0:T(8,128)(2,1)} %all-gather.10.cloned.1.call-done) | copy-start | bytes 6291460
  40.4 5.5 %copy-start.2 = (bf16[128,768]{1,0:T(8,128)(2,1)S(1)}, bf16[128,768]{1,0:T(8,128)(2,1)}, u32[]{:S(2)}) copy-start(bf16[128,768]{1,0:T(8,128)(2,1)} %param.8) | copy-start | bytes 589828
  40.4 6.4 %copy-start.4 = (s32[8]{0:T(128)S(1)}, s32[8]{0:T(128)}, u32[]{:S(2)}) copy-start(s32[8]{0:T(128)} %param.15) | copy-start | bytes 100
  40.4 6.4 %copy-start.3 = (s32[8,2]{0,1:T(2,128)S(1)}, s32[8,2]{0,1:T(2,128)}, u32[]{:S(2)}) copy-start(s32[8,2]{0,1:T(2,128)} %param.14) | copy-start | bytes 196
  40.4 208.3 %all-gather.14.cloned.1.call-start = ((), (), s32[]{:S(2)}) async-start(), calls=%async_computation.4 | async-start | bytes 3538944 | tf_op jit(solution)/shard_map/all_gather | solution.py:68
  195.9 2.7 copy-start
  259.0 1.4 copy-start.1
Sparse Core Ops, SparseCore 0:
  8.9 25.2 all-gather.9
  36.4 44.1 all-gather.7
  82.7 44.0 all-gather.5
  128.9 58.6 all-gather.11
  189.6 59.0 all-gather.13
where the time goes:
time: 269 us
  waiting for transfers between devices  209 us (78%)
  matrix products  23.8 us (9%)
  local copies, waits for them, and re-layouts  18.9 us (7%)
  between operations  13.3 us (5%)
  other arithmetic  3.51 us (1%)
    all_gather x1, waiting for transfers between devices, per_device(): every_key = lax.all_gather(text_keys, 'tm', axis=0, tiled=True)  58.6 us
    all_gather x1, waiting for transfers between devices, per_device(): every_value = lax.all_gather(text_values, 'tm', axis=0, tiled=True)  48.8 us
    all_gather x1, waiting for transfers between devices, per_device(): lax.all_gather(video_k, 'tm', axis=0, tiled=True)  43.6 us
    all_gather x1, waiting for transfers between devices, per_device(): lax.all_gather(video_v, 'tm', axis=0, tiled=True)  32.2 us
    all_gather x1, waiting for transfers between devices, per_device(): caption_block = lax.all_gather(captions, 'head', axis=0, tiled=True)  24.4 us
    dot_general x2, matrix products, absorb(): jnp.einsum('thn,nhd->thd', weights.astype(jnp.bfloat16), value_heads, pre...  6.61 us
    dot_general x1, matrix products, per_device(): jnp.dot(caption_block, text_k_weight, preferred_element_type=jnp.float32)  6.11 us
    unnamed x14, local copies, waits for them, and re-layouts  6.1 us
  transfers between devices with their start and end apart: 5, of which 5 were waited for; matrix products, arithmetic and copies ran while one was open for 11% of the time, Pallas kernels for 0%

commit v1 on v0

--- a/solution.py
+++ b/solution.py
@@ -1,15 +1,18 @@
+import functools
 import math
 
 import jax
 import jax.numpy as jnp
 from jax import lax
+from jax.experimental import pallas as pl
+from jax.experimental.pallas import tpu as pltpu
 from jax.sharding import PartitionSpec as P
 
 HD = 128
 SHOTS = 8
 
 
-def per_device(
+def gathered_form(
     video_q, video_k, video_v, captions, text_k_weight, text_v_weight, shot_spans, caption_lens
 ):
     tok_rows = video_q.shape[0]
@@ -82,6 +85,440 @@
     return (run_num / run_sum[:, :, None]).astype(jnp.bfloat16).reshape(tok_rows, -1)
 
 
+ZL = 4
+CHUNKS = 4
+MESH = pl.DeviceIdType.MESH
+
+
+def line_order(z, step):
+    inner = jnp.where(step == 0, 3, jnp.where(step == 1, 0, jnp.where(step == 2, 2, 1)))
+    return jnp.where(z == 0, 3 - step, jnp.where(z == 1, inner, jnp.where(z == 2, 3 - inner, step)))
+
+
+def merged_kernel(
+    q_ref, k_ref, v_ref, cap_ref, wk_hbm, wv_hbm, spans_ref, lens_ref, out_ref,
+    q_all, cap_all, w_all, acc, tk, v_t, row_shot, bias,
+    part, stat, x_part, x_stat, up_part, up_stat, down_part, down_stat, go_part, go_stat,
+    w_sem, own_sem, cap_y_send, cap_y_recv, cap_s_send, cap_s_recv, cap_f_send, cap_f_recv,
+    q_recv, q_up_send, q_down_send, q_x_send,
+    x_send, x_recv, xs_send, xs_recv,
+    z_send, zs_send, up_recv, ups_recv, down_recv, downs_recv,
+):
+    rows, width = q_ref.shape
+    heads = width // HD
+    cap_rows = cap_ref.shape[0]
+    text_rows = 4 * cap_rows
+    depth = cap_ref.shape[1]
+    chunk = depth // CHUNKS
+    keys = rows + text_rows
+
+    tm = lax.axis_index("tm")
+    head = lax.axis_index("head")
+    x = lax.rem(tm, 2)
+    z = lax.div(tm, 2)
+    core = lax.rem(head, 2)
+    y = lax.div(head, 2)
+    across_x = (tm + 1 - 2 * x, head)
+    above = (tm + 2, head)
+    below = (tm - 2, head)
+    sib_head = head + 1 - 2 * core
+    y_head = head + 2 - 4 * y
+    far_head = sib_head + 2 - 4 * y
+    sibling = (tm, sib_head)
+    across_y = (tm, y_head)
+
+    def columns(j):
+        return pl.ds(j * chunk, chunk)
+
+    def weight_copies(j):
+        return (
+            pltpu.make_async_copy(
+                wk_hbm.at[columns(j), :], w_all.at[columns(j), pl.ds(0, width)], w_sem.at[0, j]
+            ),
+            pltpu.make_async_copy(
+                wv_hbm.at[columns(j), :], w_all.at[columns(j), pl.ds(width, width)], w_sem.at[1, j]
+            ),
+        )
+
+    def own_caption(j):
+        return pltpu.make_async_copy(
+            cap_ref.at[:, columns(j)], cap_all.at[j, head], own_sem.at[j]
+        )
+
+    def cap_to_y(j):
+        return pltpu.make_async_remote_copy(
+            cap_ref.at[:, columns(j)], cap_all.at[j, head], cap_y_send.at[j], cap_y_recv.at[j],
+            device_id=across_y, device_id_type=MESH,
+        )
+
+    def cap_to_sibling(j):
+        return pltpu.make_async_remote_copy(
+            cap_ref.at[:, columns(j)], cap_all.at[j, head], cap_s_send.at[j], cap_s_recv.at[j],
+            device_id=sibling, device_id_type=MESH,
+        )
+
+    def cap_handed_on(j):
+        return pltpu.make_async_remote_copy(
+            cap_all.at[j, y_head], cap_all.at[j, y_head], cap_f_send.at[j], cap_f_recv.at[j],
+            device_id=sibling, device_id_type=MESH,
+        )
+
+    def q_copy(source, slot, send, device):
+        return pltpu.make_async_remote_copy(
+            source, q_all.at[slot], send, q_recv.at[slot], device_id=device, device_id_type=MESH
+        )
+
+    barrier = pltpu.get_barrier_semaphore()
+    for device in (across_x, sibling, across_y):
+        pl.semaphore_signal(barrier, inc=1, device_id=device, device_id_type=MESH)
+
+    @pl.when(z < ZL - 1)
+    def _():
+        pl.semaphore_signal(barrier, inc=1, device_id=above, device_id_type=MESH)
+
+    @pl.when(z > 0)
+    def _():
+        pl.semaphore_signal(barrier, inc=1, device_id=below, device_id_type=MESH)
+
+    for j in range(CHUNKS):
+        for copy in weight_copies(j):
+            copy.start()
+        own_caption(j).start()
+    q_own = pltpu.make_async_copy(q_ref, q_all.at[tm], own_sem.at[CHUNKS])
+    q_own.start()
+
+    pl.semaphore_wait(barrier, jnp.where((z == 0) | (z == ZL - 1), 4, 5))
+
+    for j in range(CHUNKS):
+        cap_to_y(j).start()
+
+    @pl.when(z < ZL - 1)
+    def _():
+        q_copy(q_ref, tm, q_up_send.at[z], above).start()
+
+    @pl.when(z > 0)
+    def _():
+        q_copy(q_ref, tm, q_down_send.at[z], below).start()
+
+    q_copy(q_ref, tm, q_x_send.at[z], across_x).start()
+    for j in range(CHUNKS):
+        cap_to_sibling(j).start()
+
+    stat[...] = jnp.ones_like(stat)
+    row = lax.broadcasted_iota(jnp.int32, (text_rows, HD), 0)
+    shot = row % SHOTS
+    slot = (tm * text_rows + row) // SHOTS
+    live = jnp.zeros((text_rows, HD), jnp.int32)
+    for s in range(SHOTS):
+        live = jnp.where(shot == s, lens_ref[s], live)
+    row_shot[...] = jnp.where(slot < live, shot, -1)
+    for h in range(heads):
+        at = slice(h * HD, (h + 1) * HD)
+        v_t[at, :rows] = v_ref[:, at].astype(jnp.float32).T.astype(jnp.bfloat16)
+
+    def q_step(k):
+        @pl.when(z >= k)
+        def _():
+            came = tm - 2 * k
+            q_copy(q_all.at[came], came, q_up_send.at[z - k], above).wait_recv()
+
+            @pl.when(z < ZL - 1)
+            def _():
+                q_copy(q_all.at[came], came, q_up_send.at[z - k], above).start()
+
+            q_copy(q_all.at[came], came, q_x_send.at[z - k], across_x).start()
+
+        @pl.when(z + k < ZL)
+        def _():
+            came = tm + 2 * k
+            q_copy(q_all.at[came], came, q_down_send.at[z + k], below).wait_recv()
+
+            @pl.when(z > 0)
+            def _():
+                q_copy(q_all.at[came], came, q_down_send.at[z + k], below).start()
+
+            q_copy(q_all.at[came], came, q_x_send.at[z + k], across_x).start()
+
+    tile = 256
+    tiles = 2 * width // tile
+
+    def hand_on(j):
+        cap_to_y(j).wait_recv()
+        cap_handed_on(j).start()
+
+    def project(j):
+        own_caption(j).wait()
+        cap_to_sibling(j).wait_recv()
+        cap_handed_on(j).wait_recv()
+        for copy in weight_copies(j):
+            copy.wait()
+
+        @pl.loop(0, tiles)
+        def _(n):
+            at = pl.ds(pl.multiple_of(n * tile, tile), tile)
+            block = cap_all[j].reshape(text_rows, chunk)
+            term = jnp.dot(block, w_all[columns(j), at], preferred_element_type=jnp.float32)
+            if j == 0:
+                acc[:, at] = term
+            else:
+                acc[:, at] += term
+
+    hand_on(0)
+    q_step(1)
+    hand_on(1)
+    project(0)
+    hand_on(2)
+    project(1)
+    q_step(2)
+    hand_on(3)
+    project(2)
+    q_step(3)
+    project(3)
+
+    tk[...] = acc[:, :width].astype(jnp.bfloat16)
+    for h in range(heads):
+        v_t[h * HD : (h + 1) * HD, rows:] = (
+            acc[:, width + h * HD : width + (h + 1) * HD].T.astype(jnp.bfloat16)
+        )
+
+    q_own.wait()
+    other_column = tm + 1 - 2 * x - 2 * z
+
+    scale = math.log2(math.e) / math.sqrt(HD)
+
+    def x_copies(to):
+        return (
+            pltpu.make_async_remote_copy(
+                part.at[to, 1 - x], x_part.at[to], x_send.at[to], x_recv.at[to],
+                device_id=across_x, device_id_type=MESH,
+            ),
+            pltpu.make_async_remote_copy(
+                stat.at[to, 1 - x], x_stat.at[to], xs_send.at[to], xs_recv.at[to],
+                device_id=across_x, device_id_type=MESH,
+            ),
+        )
+
+    @pl.loop(0, ZL)
+    def _(step):
+        to = line_order(z, step)
+        came = other_column + 2 * to
+        q_copy(q_all.at[came], came, q_x_send.at[0], across_x).wait_recv()
+        token = to * 2 * rows + lax.broadcasted_iota(jnp.int32, (8, 2 * rows), 1)
+        token_shot = jnp.zeros((8, 2 * rows), jnp.int32)
+        for s in range(SHOTS):
+            inside = (token >= spans_ref[s, 0]) & (token < spans_ref[s, 1])
+            token_shot = jnp.where(inside, s, token_shot)
+        of_token = token_shot[:1]
+        for half in range(2):
+            at = slice(half * rows, (half + 1) * rows)
+            bias[:, at] = jnp.where(row_shot[...] == of_token[:, at], 0.0, -jnp.inf)
+        for h in range(heads):
+            at = slice(h * HD, (h + 1) * HD)
+            queries = q_all[pl.ds(2 * to, 2), :, at].reshape(2 * rows, HD)
+            dims = (((1,), (1,)), ((), ()))
+            video = scale * lax.dot_general(
+                k_ref[:, at], queries, dims, preferred_element_type=jnp.float32
+            )
+            text = (
+                scale
+                * lax.dot_general(tk[:, at], queries, dims, preferred_element_type=jnp.float32)
+                + bias[...]
+            )
+            top = jnp.maximum(
+                jnp.max(video, axis=0, keepdims=True), jnp.max(text, axis=0, keepdims=True)
+            )
+            video = jnp.exp2(video - top)
+            text = jnp.exp2(text - top)
+            total = jnp.sum(video, axis=0, keepdims=True) + jnp.sum(text, axis=0, keepdims=True)
+            mixed = jnp.dot(
+                v_t[at, :rows], video.astype(jnp.bfloat16), preferred_element_type=jnp.float32
+            ) + jnp.dot(
+                v_t[at, rows:], text.astype(jnp.bfloat16), preferred_element_type=jnp.float32
+            )
+            for half in range(2):
+                lanes = slice(half * rows, (half + 1) * rows)
+                part[to, half, at, :] = mixed[:, lanes].astype(jnp.bfloat16)
+                stat[to, half, h : h + 1, :] = top[:, lanes]
+                stat[to, half, 8 + h : 9 + h, :] = total[:, lanes]
+        for copy in x_copies(to):
+            copy.start()
+
+    def z_copies(to, device, into_part, into_stat, recv, recv_stat):
+        return (
+            pltpu.make_async_remote_copy(
+                go_part.at[to], into_part.at[to], z_send.at[to], recv.at[to],
+                device_id=device, device_id_type=MESH,
+            ),
+            pltpu.make_async_remote_copy(
+                go_stat.at[to], into_stat.at[to], zs_send.at[to], recv_stat.at[to],
+                device_id=device, device_id_type=MESH,
+            ),
+        )
+
+    def up_copies(to):
+        return z_copies(to, above, up_part, up_stat, up_recv, ups_recv)
+
+    def down_copies(to):
+        return z_copies(to, below, down_part, down_stat, down_recv, downs_recv)
+
+    def merge(to, sources, last=False):
+        tops = [s[to, 0:8, :] for _, s in sources]
+        top = functools.reduce(jnp.maximum, tops)
+        factors = [jnp.exp2(t - top) for t in tops]
+        total = sum(f * s[to, 8:16, :] for f, (_, s) in zip(factors, sources))
+        if last:
+            factors = [f / total for f in factors]
+        else:
+            go_stat[to, 0:8, :] = top
+            go_stat[to, 8:16, :] = total
+        for h in range(heads):
+            at = slice(h * HD, (h + 1) * HD)
+            mixed = sum(
+                f[h : h + 1, :] * p[to, at, :].astype(jnp.float32)
+                for f, (p, _) in zip(factors, sources)
+            )
+            if last:
+                out_ref[:, at] = mixed.T.astype(jnp.bfloat16)
+            else:
+                go_part[to, at, :] = mixed.astype(jnp.bfloat16)
+
+    own = (part.at[:, x], stat.at[:, x])
+    over_x = (x_part, x_stat)
+    from_below = (up_part, up_stat)
+    from_above = (down_part, down_stat)
+
+    @pl.loop(0, ZL)
+    def _(step):
+        to = line_order(z, step)
+        for copy in x_copies(to):
+            copy.wait_recv()
+
+        @pl.when((to >= z) & (z > 0))
+        def _():
+            for copy in up_copies(to):
+                copy.wait_recv()
+
+        @pl.when((to <= z) & (z < ZL - 1))
+        def _():
+            for copy in down_copies(to):
+                copy.wait_recv()
+
+        @pl.when(to > z)
+        def _():
+            @pl.when(z > 0)
+            def _():
+                merge(to, [own, over_x, from_below])
+
+            @pl.when(z == 0)
+            def _():
+                merge(to, [own, over_x])
+
+            for copy in up_copies(to):
+                copy.start()
+
+        @pl.when(to < z)
+        def _():
+            @pl.when(z < ZL - 1)
+            def _():
+                merge(to, [own, over_x, from_above])
+
+            @pl.when(z == ZL - 1)
+            def _():
+                merge(to, [own, over_x])
+
+            for copy in down_copies(to):
+                copy.start()
+
+        @pl.when(to == z)
+        def _():
+            @pl.when(z == 0)
+            def _():
+                merge(to, [own, over_x, from_above], last=True)
+
+            @pl.when(z == ZL - 1)
+            def _():
+                merge(to, [own, over_x, from_below], last=True)
+
+            @pl.when((z > 0) & (z < ZL - 1))
+            def _():
+                merge(to, [own, over_x, from_below, from_above], last=True)
+
+    for j in range(CHUNKS):
+        cap_to_y(j).wait_send()
+        cap_to_sibling(j).wait_send()
+        cap_handed_on(j).wait_send()
+    for b in range(ZL):
+        slot_b = x + 2 * b
+
+        @pl.when((b <= z) & (z < ZL - 1))
+        def _():
+            q_copy(q_all.at[slot_b], slot_b, q_up_send.at[b], above).wait_send()
+
+        @pl.when((b >= z) & (z > 0))
+        def _():
+            q_copy(q_all.at[slot_b], slot_b, q_down_send.at[b], below).wait_send()
+
+        q_copy(q_all.at[slot_b], slot_b, q_x_send.at[b], across_x).wait_send()
+        for copy in x_copies(b):
+            copy.wait_send()
+
+        @pl.when(b > z)
+        def _():
+            for copy in up_copies(b):
+                copy.wait_send()
+
+        @pl.when(b < z)
+        def _():
+            for copy in down_copies(b):
+                copy.wait_send()
+
+
+def merged_form(
+    video_q, video_k, video_v, captions, text_k_weight, text_v_weight, shot_spans, caption_lens
+):
+    rows, width = video_q.shape
+    cap_rows, depth = captions.shape
+    text_rows = 4 * cap_rows
+    vmem = pl.BlockSpec(memory_space=pltpu.VMEM)
+    smem = pl.BlockSpec(memory_space=pltpu.SMEM)
+    hbm = pl.BlockSpec(memory_space=pl.ANY)
+    bf16, f32 = jnp.bfloat16, jnp.float32
+    dma = pltpu.SemaphoreType.DMA
+    blocks = pltpu.VMEM((ZL, width, rows), bf16)
+    stats = pltpu.VMEM((ZL, 16, rows), f32)
+    return pl.pallas_call(
+        merged_kernel,
+        out_shape=jax.ShapeDtypeStruct((rows, width), bf16),
+        in_specs=[vmem, vmem, vmem, vmem, hbm, hbm, smem, smem],
+        out_specs=vmem,
+        scratch_shapes=[
+            pltpu.VMEM((2 * ZL, rows, width), bf16),
+            pltpu.VMEM((CHUNKS, 4, cap_rows, depth // CHUNKS), bf16),
+            pltpu.VMEM((depth, 2 * width), bf16),
+            pltpu.VMEM((text_rows, 2 * width), f32),
+            pltpu.VMEM((text_rows, width), bf16),
+            pltpu.VMEM((width, rows + text_rows), bf16),
+            pltpu.VMEM((text_rows, HD), jnp.int32),
+            pltpu.VMEM((text_rows, 2 * rows), f32),
+            pltpu.VMEM((ZL, 2, width, rows), bf16),
+            pltpu.VMEM((ZL, 2, 16, rows), f32),
+            blocks, stats, blocks, stats, blocks, stats, blocks, stats,
+            dma((2, CHUNKS)),
+            dma((CHUNKS + 1,)),
+        ]
+        + [dma((CHUNKS,))] * 6
+        + [dma((2 * ZL,))]
+        + [dma((ZL,))] * 3
+        + [dma((ZL,))] * 4
+        + [dma((ZL,))] * 6,
+        compiler_params=pltpu.CompilerParams(
+            collective_id=0, has_side_effects=True, vmem_limit_bytes=48 << 20
+        ),
+    )(
+        video_q, video_k, video_v, captions, text_k_weight, text_v_weight, shot_spans, caption_lens
+    )
+
+
 def solution(mesh):
     placed = (
         P("tm", "head"),
@@ -93,6 +530,8 @@
         P(),
         P(),
     )
+    fits = mesh.shape["tm"] == 2 * ZL and mesh.shape["head"] == 4
+    per_device = merged_form if fits else gathered_form
     return jax.shard_map(
         per_device, mesh=mesh, in_specs=placed, out_specs=P("tm", "head"), check_vma=False
     )

time: 269 us -> 60.8 us (0.23)
  waiting for transfers between devices: 209 us -> 0 us
  Pallas kernels: 0 us -> 54.6 us
  matrix products: 23.8 us -> 0 us
  between operations: 13.3 us -> 0.01 us
  local copies, waits for them, and re-layouts: 18.9 us -> 5.91 us
  other arithmetic: 3.51 us -> 0 us
    all_gather x5 -> x0, waiting for transfers between devices: 208 us -> none  [the longest x1 58.6 us: per_device(): every_key = lax.all_gather(text_keys, 'tm', axis=0, tiled=True)]
    pallas_call x0 -> x1, Pallas kernels: none -> 54.6 us  [merged_form(): pl.pallas_call(merged_kernel, out_shape=jax.ShapeDtypeStruct((rows, width...]
    dot_general x6 -> x0, matrix products: 23.8 us -> none  [the longest x2 6.61 us: absorb(): jnp.einsum('thn,nhd->thd', weights.astype(jnp.bfloat16), value_heads, pre...]
    all_gather x3 -> x0, local copies, waits for them, and re-layouts: 12 us -> none  [the longest x1 4.74 us: per_device(): every_key = lax.all_gather(text_keys, 'tm', axis=0, tiled=True)]
    unnamed x14 -> x12, local copies, waits for them, and re-layouts: 6.1 us -> 5.91 us
  transfers between devices with their start and end apart: 5 -> 0, of which waited for: 5 -> 0; matrix products, arithmetic and copies ran while one was open for 11% -> 0% of each run, Pallas kernels for 0% -> 0%
where the time goes in v1:
time: 60.8 us; the launch traced here: 60.5 us
  Pallas kernels  54.6 us (90%)
  local copies, waits for them, and re-layouts  5.91 us (10%)
    pallas_call x1, Pallas kernels, merged_form(): pl.pallas_call(merged_kernel, out_shape=jax.ShapeDtypeStruct((rows, width...  54.6 us
    unnamed x12, local copies, waits for them, and re-layouts  5.91 us

profile of v1, /device:TPU:0, one launch (start us, length us, event | category | flops | bytes accessed | tf_op | source)
XLA Modules:
  0.0 60.5 jit_solution(16361016498279768744)
XLA Ops:
  0.0 0.8 %copy.9.spans_ref = s32[8,2]{1,0:T(8,128)S(1)} copy(s32[8,2]{0,1:T(2,128)} %param.14) | data formatting | bytes 128 | tf_op args[6]
  0.8 0.0 copy-start
  0.8 1.0 %copy-done = bf16[64,4096]{1,0:T(8,128)(2,1)S(1)} copy-done((bf16[64,4096]{1,0:T(8,128)(2,1)S(1)}, bf16[64,4096]{1,0:T(8,128)(2,1)}, u32[]{:S(2)}) %copy-start) | copy-done | bytes 524312
  1.8 0.0 copy-start.1
  1.8 0.9 %copy-done.1 = bf16[128,768]{1,0:T(8,128)(2,1)S(1)} copy-done((bf16[128,768]{1,0:T(8,128)(2,1)S(1)}, bf16[128,768]{1,0:T(8,128)(2,1)}, u32[]{:S(2)}) %copy-start.1) | copy-done | bytes 196632
  2.7 0.0 copy-start.2
  2.7 0.9 %copy-done.2 = bf16[128,768]{1,0:T(8,128)(2,1)S(1)} copy-done((bf16[128,768]{1,0:T(8,128)(2,1)S(1)}, bf16[128,768]{1,0:T(8,128)(2,1)}, u32[]{:S(2)}) %copy-start.2) | copy-done | bytes 196632
  3.7 0.0 copy-start.3
  3.7 0.9 %copy-done.3 = bf16[128,768]{1,0:T(8,128)(2,1)S(1)} copy-done((bf16[128,768]{1,0:T(8,128)(2,1)S(1)}, bf16[128,768]{1,0:T(8,128)(2,1)}, u32[]{:S(2)}) %copy-start.3) | copy-done | bytes 196632
  4.6 0.0 copy-start.4
  4.6 0.7 %copy-done.4 = s32[8]{0:T(128)S(1)} copy-done((s32[8]{0:T(128)S(1)}, s32[8]{0:T(128)}, u32[]{:S(2)}) %copy-start.4) | copy-done | bytes 56
  5.2 54.6 %shard_map.82 = bf16[128,768]{1,0:T(8,128)(2,1)S(1)} custom-call(bf16[128,768]{1,0:T(8,128)(2,1)S(1)} %copy-done.1, bf16[128,768]{1,0:T(8,128)(2,1)S(1)} %copy-done.2, bf16[128,768]{1,0:T(8,128)(2,1)S(1)} %copy-done.3, bf16[64,4096]{1,0:T(8,128)(2,1)S(1)} %copy-done, bf16[4096,768]{1,0:T(8,128)(2,1)} %wk_hbm.1, bf16[4096,768]{1,0:T(8,128)(2,1)} %wv_hbm.1, ...), custom_call_target="tpu_custom_call" | custom-call | tf_op jit(solution)/shard_map/pallas_call | solution.py:489
  59.8 0.7 %copy.11 = bf16[128,768]{1,0:T(8,128)(2,1)} copy(bf16[128,768]{1,0:T(8,128)(2,1)S(1)} %shard_map.82) | data formatting | bytes 393216
Async XLA Ops:
  0.8 1.0 %copy-start = (bf16[64,4096]{1,0:T(8,128)(2,1)S(1)}, bf16[64,4096]{1,0:T(8,128)(2,1)}, u32[]{:S(2)}) copy-start(bf16[64,4096]{1,0:T(8,128)(2,1)} %cap_ref.1) | copy-start | bytes 1572868
  1.8 0.9 %copy-start.1 = (bf16[128,768]{1,0:T(8,128)(2,1)S(1)}, bf16[128,768]{1,0:T(8,128)(2,1)}, u32[]{:S(2)}) copy-start(bf16[128,768]{1,0:T(8,128)(2,1)} %q_ref.1) | copy-start | bytes 589828
  2.7 0.9 %copy-start.2 = (bf16[128,768]{1,0:T(8,128)(2,1)S(1)}, bf16[128,768]{1,0:T(8,128)(2,1)}, u32[]{:S(2)}) copy-start(bf16[128,768]{1,0:T(8,128)(2,1)} %k_ref.1) | copy-start | bytes 589828
  3.7 0.9 %copy-start.3 = (bf16[128,768]{1,0:T(8,128)(2,1)S(1)}, bf16[128,768]{1,0:T(8,128)(2,1)}, u32[]{:S(2)}) copy-start(bf16[128,768]{1,0:T(8,128)(2,1)} %v_ref.1) | copy-start | bytes 589828
  4.6 0.7 %copy-start.4 = (s32[8]{0:T(128)S(1)}, s32[8]{0:T(128)}, u32[]{:S(2)}) copy-start(s32[8]{0:T(128)} %lens_ref.1) | copy-start | bytes 100

commit v2 on v1

--- a/solution.py
+++ b/solution.py
@@ -96,7 +96,8 @@
 
 
 def merged_kernel(
-    q_ref, k_ref, v_ref, cap_ref, wk_hbm, wv_hbm, spans_ref, lens_ref, out_ref,
+    q_ref, k_hbm, v_hbm, cap_ref, wk_hbm, wv_hbm, spans_ref, lens_ref, out_ref,
+    k_ref, v_ref,
     q_all, cap_all, w_all, acc, tk, v_t, row_shot, bias,
     part, stat, x_part, x_stat, up_part, up_stat, down_part, down_stat, go_part, go_stat,
     w_sem, own_sem, cap_y_send, cap_y_recv, cap_s_send, cap_s_recv, cap_f_send, cap_f_recv,
@@ -186,6 +187,10 @@
         own_caption(j).start()
     q_own = pltpu.make_async_copy(q_ref, q_all.at[tm], own_sem.at[CHUNKS])
     q_own.start()
+    k_own = pltpu.make_async_copy(k_hbm, k_ref, own_sem.at[CHUNKS + 1])
+    k_own.start()
+    v_own = pltpu.make_async_copy(v_hbm, v_ref, own_sem.at[CHUNKS + 2])
+    v_own.start()
 
     pl.semaphore_wait(barrier, jnp.where((z == 0) | (z == ZL - 1), 4, 5))
 
@@ -212,6 +217,7 @@
     for s in range(SHOTS):
         live = jnp.where(shot == s, lens_ref[s], live)
     row_shot[...] = jnp.where(slot < live, shot, -1)
+    v_own.wait()
     for h in range(heads):
         at = slice(h * HD, (h + 1) * HD)
         v_t[at, :rows] = v_ref[:, at].astype(jnp.float32).T.astype(jnp.bfloat16)
@@ -282,6 +288,7 @@
         )
 
     q_own.wait()
+    k_own.wait()
     other_column = tm + 1 - 2 * x - 2 * z
 
     scale = math.log2(math.e) / math.sqrt(HD)
@@ -306,7 +313,7 @@
         token = to * 2 * rows + lax.broadcasted_iota(jnp.int32, (8, 2 * rows), 1)
         token_shot = jnp.zeros((8, 2 * rows), jnp.int32)
         for s in range(SHOTS):
-            inside = (token >= spans_ref[s, 0]) & (token < spans_ref[s, 1])
+            inside = (token >= spans_ref[0, s]) & (token < spans_ref[1, s])
             token_shot = jnp.where(inside, s, token_shot)
         of_token = token_shot[:1]
         for half in range(2):
@@ -481,7 +488,7 @@
     text_rows = 4 * cap_rows
     vmem = pl.BlockSpec(memory_space=pltpu.VMEM)
     smem = pl.BlockSpec(memory_space=pltpu.SMEM)
-    hbm = pl.BlockSpec(memory_space=pl.ANY)
+    hbm = pl.BlockSpec(memory_space=pltpu.HBM)
     bf16, f32 = jnp.bfloat16, jnp.float32
     dma = pltpu.SemaphoreType.DMA
     blocks = pltpu.VMEM((ZL, width, rows), bf16)
@@ -489,9 +496,11 @@
     return pl.pallas_call(
         merged_kernel,
         out_shape=jax.ShapeDtypeStruct((rows, width), bf16),
-        in_specs=[vmem, vmem, vmem, vmem, hbm, hbm, smem, smem],
+        in_specs=[hbm, hbm, hbm, hbm, hbm, hbm, smem, smem],
         out_specs=vmem,
         scratch_shapes=[
+            pltpu.VMEM((rows, width), bf16),
+            pltpu.VMEM((rows, width), bf16),
             pltpu.VMEM((2 * ZL, rows, width), bf16),
             pltpu.VMEM((CHUNKS, 4, cap_rows, depth // CHUNKS), bf16),
             pltpu.VMEM((depth, 2 * width), bf16),
@@ -504,7 +513,7 @@
             pltpu.VMEM((ZL, 2, 16, rows), f32),
             blocks, stats, blocks, stats, blocks, stats, blocks, stats,
             dma((2, CHUNKS)),
-            dma((CHUNKS + 1,)),
+            dma((CHUNKS + 3,)),
         ]
         + [dma((CHUNKS,))] * 6
         + [dma((2 * ZL,))]
@@ -512,10 +521,10 @@
         + [dma((ZL,))] * 4
         + [dma((ZL,))] * 6,
         compiler_params=pltpu.CompilerParams(
-            collective_id=0, has_side_effects=True, vmem_limit_bytes=48 << 20
+            collective_id=0, has_side_effects=True, vmem_limit_bytes=63 << 20
         ),
     )(
-        video_q, video_k, video_v, captions, text_k_weight, text_v_weight, shot_spans, caption_lens
+        video_q, video_k, video_v, captions, text_k_weight, text_v_weight, shot_spans.T, caption_lens
     )
 
 

time: 60.8 us -> 57.4 us (0.944)
  local copies, waits for them, and re-layouts: 5.91 us -> 1.62 us
  Pallas kernels: 54.6 us -> 55.6 us
    unnamed x12 -> x1, local copies, waits for them, and re-layouts: 5.91 us -> 1.62 us
    pallas_call x1, Pallas kernels: 54.6 us -> 55.6 us  [merged_form(): pl.pallas_call(merged_kernel, out_shape=jax.ShapeDtypeStruct((rows, width...]
where the time goes in v2:
time: 57.4 us; the launch traced here: 57.2 us
  Pallas kernels  55.6 us (97%)
  local copies, waits for them, and re-layouts  1.62 us (3%)
    pallas_call x1, Pallas kernels, merged_form(): pl.pallas_call(merged_kernel, out_shape=jax.ShapeDtypeStruct((rows, width...  55.6 us
    unnamed x1, local copies, waits for them, and re-layouts  1.62 us

profile of v2, /device:TPU:0, one launch (start us, length us, event | category | flops | bytes accessed | tf_op | source)
XLA Modules:
  0.0 57.2 jit_solution(11714140701955083368)
XLA Ops:
  0.0 55.6 %shard_map.82 = bf16[128,768]{1,0:T(8,128)(2,1)} custom-call(bf16[128,768]{1,0:T(8,128)(2,1)} %q_ref.1, bf16[128,768]{1,0:T(8,128)(2,1)} %k_hbm.1, bf16[128,768]{1,0:T(8,128)(2,1)} %v_hbm.1, bf16[64,4096]{1,0:T(8,128)(2,1)} %cap_ref.1, bf16[4096,768]{1,0:T(8,128)(2,1)} %wk_hbm.1, bf16[4096,768]{1,0:T(8,128)(2,1)} %wv_hbm.1, s32[2,8]{1,0:T(2,128)} %bitcast.1, ...), custom_call_target="tpu_custom_call" | custom-call | tf_op jit(solution)/shard_map/pallas_call | solution.py:496
  55.6 1.6 %copy.10 = bf16[128,768]{1,0:T(8,128)(2,1)} copy(bf16[128,768]{1,0:T(8,128)(2,1)} %shard_map.82) | data formatting | bytes 393216

commit v3 on v2

--- a/solution.py
+++ b/solution.py
@@ -87,6 +87,7 @@
 
 ZL = 4
 CHUNKS = 4
+GROUPS = 2
 MESH = pl.DeviceIdType.MESH
 
 
@@ -102,6 +103,7 @@
     part, stat, x_part, x_stat, up_part, up_stat, down_part, down_stat, go_part, go_stat,
     w_sem, own_sem, cap_y_send, cap_y_recv, cap_s_send, cap_s_recv, cap_f_send, cap_f_recv,
     q_recv, q_up_send, q_down_send, q_x_send,
+    q_half_send, q_half_recv,
     x_send, x_recv, xs_send, xs_recv,
     z_send, zs_send, up_recv, ups_recv, down_recv, downs_recv,
 ):
@@ -169,6 +171,24 @@
             source, q_all.at[slot], send, q_recv.at[slot], device_id=device, device_id_type=MESH
         )
 
+    half_rows = rows // 2
+    odd = lax.rem(z, 2)
+    partner_z = z + 1 - 2 * odd
+    partner = (tm + 2 - 4 * odd, head)
+
+    def q_x_half(slot, b):
+        lower = q_all.at[slot, pl.ds(0, half_rows)]
+        return pltpu.make_async_remote_copy(
+            lower, lower, q_x_send.at[b], q_recv.at[slot], device_id=across_x, device_id_type=MESH
+        )
+
+    def q_round(slot):
+        upper = q_all.at[slot, pl.ds(half_rows, half_rows)]
+        return pltpu.make_async_remote_copy(
+            upper, upper, q_half_send.at[0], q_half_recv.at[0],
+            device_id=partner, device_id_type=MESH,
+        )
+
     barrier = pltpu.get_barrier_semaphore()
     for device in (across_x, sibling, across_y):
         pl.semaphore_signal(barrier, inc=1, device_id=device, device_id_type=MESH)
@@ -232,7 +252,16 @@
             def _():
                 q_copy(q_all.at[came], came, q_up_send.at[z - k], above).start()
 
-            q_copy(q_all.at[came], came, q_x_send.at[z - k], across_x).start()
+            if k == 1:
+                @pl.when(odd == 1)
+                def _():
+                    q_x_half(came, z - k).start()
+
+                @pl.when(jnp.logical_not(odd == 1))
+                def _():
+                    q_copy(q_all.at[came], came, q_x_send.at[z - k], across_x).start()
+            else:
+                q_copy(q_all.at[came], came, q_x_send.at[z - k], across_x).start()
 
         @pl.when(z + k < ZL)
         def _():
@@ -243,7 +272,21 @@
             def _():
                 q_copy(q_all.at[came], came, q_down_send.at[z + k], below).start()
 
-            q_copy(q_all.at[came], came, q_x_send.at[z + k], across_x).start()
+            if k == 1:
+                @pl.when(odd == 0)
+                def _():
+                    q_x_half(came, z + k).start()
+
+                @pl.when(jnp.logical_not(odd == 0))
+                def _():
+                    q_copy(q_all.at[came], came, q_x_send.at[z + k], across_x).start()
+            else:
+                q_copy(q_all.at[came], came, q_x_send.at[z + k], across_x).start()
+
+        if k == 1:
+            beside = tm + 1 - 2 * x
+            q_copy(q_all.at[beside], beside, q_x_send.at[z], across_x).wait_recv()
+            q_round(beside).start()
 
     tile = 256
     tiles = 2 * width // tile
@@ -293,14 +336,20 @@
 
     scale = math.log2(math.e) / math.sqrt(HD)
 
-    def x_copies(to):
+    group = heads // GROUPS
+
+    def of_group(g):
+        return pl.ds(g * group * HD, group * HD)
+
+    def x_copies(to, g):
         return (
             pltpu.make_async_remote_copy(
-                part.at[to, 1 - x], x_part.at[to], x_send.at[to], x_recv.at[to],
+                part.at[to, 1 - x, of_group(g)], x_part.at[to, of_group(g)],
+                x_send.at[to, g], x_recv.at[to, g],
                 device_id=across_x, device_id_type=MESH,
             ),
             pltpu.make_async_remote_copy(
-                stat.at[to, 1 - x], x_stat.at[to], xs_send.at[to], xs_recv.at[to],
+                stat.at[to, 1 - x, g], x_stat.at[to, g], xs_send.at[to, g], xs_recv.at[to, g],
                 device_id=across_x, device_id_type=MESH,
             ),
         )
@@ -309,7 +358,16 @@
     def _(step):
         to = line_order(z, step)
         came = other_column + 2 * to
-        q_copy(q_all.at[came], came, q_x_send.at[0], across_x).wait_recv()
+
+        @pl.when(to == partner_z)
+        def _():
+            q_x_half(came, 0).wait_recv()
+            q_round(came).wait_recv()
+
+        @pl.when((to != partner_z) & (to != z))
+        def _():
+            q_copy(q_all.at[came], came, q_x_send.at[0], across_x).wait_recv()
+
         token = to * 2 * rows + lax.broadcasted_iota(jnp.int32, (8, 2 * rows), 1)
         token_shot = jnp.zeros((8, 2 * rows), jnp.int32)
         for s in range(SHOTS):
@@ -320,6 +378,7 @@
             at = slice(half * rows, (half + 1) * rows)
             bias[:, at] = jnp.where(row_shot[...] == of_token[:, at], 0.0, -jnp.inf)
         for h in range(heads):
+            g, r = h // group, h % group
             at = slice(h * HD, (h + 1) * HD)
             queries = q_all[pl.ds(2 * to, 2), :, at].reshape(2 * rows, HD)
             dims = (((1,), (1,)), ((), ()))
@@ -345,43 +404,46 @@
             for half in range(2):
                 lanes = slice(half * rows, (half + 1) * rows)
                 part[to, half, at, :] = mixed[:, lanes].astype(jnp.bfloat16)
-                stat[to, half, h : h + 1, :] = top[:, lanes]
-                stat[to, half, 8 + h : 9 + h, :] = total[:, lanes]
-        for copy in x_copies(to):
-            copy.start()
-
-    def z_copies(to, device, into_part, into_stat, recv, recv_stat):
+                stat[to, half, g, r : r + 1, :] = top[:, lanes]
+                stat[to, half, g, 8 + r : 9 + r, :] = total[:, lanes]
+            if r == group - 1:
+                for copy in x_copies(to, g):
+                    copy.start()
+
+    def z_copies(to, g, device, into_part, into_stat, recv, recv_stat):
         return (
             pltpu.make_async_remote_copy(
-                go_part.at[to], into_part.at[to], z_send.at[to], recv.at[to],
+                go_part.at[to, of_group(g)], into_part.at[to, of_group(g)],
+                z_send.at[to, g], recv.at[to, g],
                 device_id=device, device_id_type=MESH,
             ),
             pltpu.make_async_remote_copy(
-                go_stat.at[to], into_stat.at[to], zs_send.at[to], recv_stat.at[to],
+                go_stat.at[to, g], into_stat.at[to, g], zs_send.at[to, g], recv_stat.at[to, g],
                 device_id=device, device_id_type=MESH,
             ),
         )
 
-    def up_copies(to):
-        return z_copies(to, above, up_part, up_stat, up_recv, ups_recv)
-
-    def down_copies(to):
-        return z_copies(to, below, down_part, down_stat, down_recv, downs_recv)
-
-    def merge(to, sources, last=False):
-        tops = [s[to, 0:8, :] for _, s in sources]
+    def up_copies(to, g):
+        return z_copies(to, g, above, up_part, up_stat, up_recv, ups_recv)
+
+    def down_copies(to, g):
+        return z_copies(to, g, below, down_part, down_stat, down_recv, downs_recv)
+
+    def merge(to, g, sources, last=False):
+        tops = [s[to, g, 0:8, :] for _, s in sources]
         top = functools.reduce(jnp.maximum, tops)
         factors = [jnp.exp2(t - top) for t in tops]
-        total = sum(f * s[to, 8:16, :] for f, (_, s) in zip(factors, sources))
+        total = sum(f * s[to, g, 8:16, :] for f, (_, s) in zip(factors, sources))
         if last:
             factors = [f / total for f in factors]
         else:
-            go_stat[to, 0:8, :] = top
-            go_stat[to, 8:16, :] = total
-        for h in range(heads):
+            go_stat[to, g, 0:8, :] = top
+            go_stat[to, g, 8:16, :] = total
+        for r in range(group):
+            h = g * group + r
             at = slice(h * HD, (h + 1) * HD)
             mixed = sum(
-                f[h : h + 1, :] * p[to, at, :].astype(jnp.float32)
+                f[r : r + 1, :] * p[to, at, :].astype(jnp.float32)
                 for f, (p, _) in zip(factors, sources)
             )
             if last:
@@ -394,66 +456,71 @@
     from_below = (up_part, up_stat)
     from_above = (down_part, down_stat)
 
+    def merge_step(to, g):
+        for copy in x_copies(to, g):
+            copy.wait_recv()
+
+        @pl.when((to >= z) & (z > 0))
+        def _():
+            for copy in up_copies(to, g):
+                copy.wait_recv()
+
+        @pl.when((to <= z) & (z < ZL - 1))
+        def _():
+            for copy in down_copies(to, g):
+                copy.wait_recv()
+
+        @pl.when(to > z)
+        def _():
+            @pl.when(z > 0)
+            def _():
+                merge(to, g, [own, over_x, from_below])
+
+            @pl.when(z == 0)
+            def _():
+                merge(to, g, [own, over_x])
+
+            for copy in up_copies(to, g):
+                copy.start()
+
+        @pl.when(to < z)
+        def _():
+            @pl.when(z < ZL - 1)
+            def _():
+                merge(to, g, [own, over_x, from_above])
+
+            @pl.when(z == ZL - 1)
+            def _():
+                merge(to, g, [own, over_x])
+
+            for copy in down_copies(to, g):
+                copy.start()
+
+        @pl.when(to == z)
+        def _():
+            @pl.when(z == 0)
+            def _():
+                merge(to, g, [own, over_x, from_above], last=True)
+
+            @pl.when(z == ZL - 1)
+            def _():
+                merge(to, g, [own, over_x, from_below], last=True)
+
+            @pl.when((z > 0) & (z < ZL - 1))
+            def _():
+                merge(to, g, [own, over_x, from_below, from_above], last=True)
+
     @pl.loop(0, ZL)
     def _(step):
         to = line_order(z, step)
-        for copy in x_copies(to):
-            copy.wait_recv()
-
-        @pl.when((to >= z) & (z > 0))
-        def _():
-            for copy in up_copies(to):
-                copy.wait_recv()
-
-        @pl.when((to <= z) & (z < ZL - 1))
-        def _():
-            for copy in down_copies(to):
-                copy.wait_recv()
-
-        @pl.when(to > z)
-        def _():
-            @pl.when(z > 0)
-            def _():
-                merge(to, [own, over_x, from_below])
-
-            @pl.when(z == 0)
-            def _():
-                merge(to, [own, over_x])
-
-            for copy in up_copies(to):
-                copy.start()
-
-        @pl.when(to < z)
-        def _():
-            @pl.when(z < ZL - 1)
-            def _():
-                merge(to, [own, over_x, from_above])
-
-            @pl.when(z == ZL - 1)
-            def _():
-                merge(to, [own, over_x])
-
-            for copy in down_copies(to):
-                copy.start()
-
-        @pl.when(to == z)
-        def _():
-            @pl.when(z == 0)
-            def _():
-                merge(to, [own, over_x, from_above], last=True)
-
-            @pl.when(z == ZL - 1)
-            def _():
-                merge(to, [own, over_x, from_below], last=True)
-
-            @pl.when((z > 0) & (z < ZL - 1))
-            def _():
-                merge(to, [own, over_x, from_below, from_above], last=True)
+        for g in range(GROUPS):
+            merge_step(to, g)
 
     for j in range(CHUNKS):
         cap_to_y(j).wait_send()
         cap_to_sibling(j).wait_send()
         cap_handed_on(j).wait_send()
+    q_round(tm + 1 - 2 * x).wait_send()
     for b in range(ZL):
         slot_b = x + 2 * b
 
@@ -465,19 +532,29 @@
         def _():
             q_copy(q_all.at[slot_b], slot_b, q_down_send.at[b], below).wait_send()
 
-        q_copy(q_all.at[slot_b], slot_b, q_x_send.at[b], across_x).wait_send()
-        for copy in x_copies(b):
-            copy.wait_send()
+        @pl.when(b == partner_z)
+        def _():
+            q_x_half(slot_b, b).wait_send()
+
+        @pl.when(b != partner_z)
+        def _():
+            q_copy(q_all.at[slot_b], slot_b, q_x_send.at[b], across_x).wait_send()
+
+        for g in range(GROUPS):
+            for copy in x_copies(b, g):
+                copy.wait_send()
 
         @pl.when(b > z)
         def _():
-            for copy in up_copies(b):
-                copy.wait_send()
+            for g in range(GROUPS):
+                for copy in up_copies(b, g):
+                    copy.wait_send()
 
         @pl.when(b < z)
         def _():
-            for copy in down_copies(b):
-                copy.wait_send()
+            for g in range(GROUPS):
+                for copy in down_copies(b, g):
+                    copy.wait_send()
 
 
 def merged_form(
@@ -492,7 +569,7 @@
     bf16, f32 = jnp.bfloat16, jnp.float32
     dma = pltpu.SemaphoreType.DMA
     blocks = pltpu.VMEM((ZL, width, rows), bf16)
-    stats = pltpu.VMEM((ZL, 16, rows), f32)
+    stats = pltpu.VMEM((ZL, GROUPS, 16, rows), f32)
     return pl.pallas_call(
         merged_kernel,
         out_shape=jax.ShapeDtypeStruct((rows, width), bf16),
@@ -510,7 +587,7 @@
             pltpu.VMEM((text_rows, HD), jnp.int32),
             pltpu.VMEM((text_rows, 2 * rows), f32),
             pltpu.VMEM((ZL, 2, width, rows), bf16),
-            pltpu.VMEM((ZL, 2, 16, rows), f32),
+            pltpu.VMEM((ZL, 2, GROUPS, 16, rows), f32),
             blocks, stats, blocks, stats, blocks, stats, blocks, stats,
             dma((2, CHUNKS)),
             dma((CHUNKS + 3,)),
@@ -518,8 +595,8 @@
         + [dma((CHUNKS,))] * 6
         + [dma((2 * ZL,))]
         + [dma((ZL,))] * 3
-        + [dma((ZL,))] * 4
-        + [dma((ZL,))] * 6,
+        + [dma((1,))] * 2
+        + [dma((ZL, GROUPS))] * 10,
         compiler_params=pltpu.CompilerParams(
             collective_id=0, has_side_effects=True, vmem_limit_bytes=63 << 20
         ),

time: 57.4 us -> 56.5 us (0.984)
  Pallas kernels: 55.6 us -> 54.7 us
    pallas_call x1, Pallas kernels: 55.6 us -> 54.7 us  [merged_form(): pl.pallas_call(merged_kernel, out_shape=jax.ShapeDtypeStruct((rows, width...]
where the time goes in v3:
time: 56.5 us; the launch traced here: 56.4 us
  Pallas kernels  54.7 us (97%)
  local copies, waits for them, and re-layouts  1.62 us (3%)
    pallas_call x1, Pallas kernels, merged_form(): pl.pallas_call(merged_kernel, out_shape=jax.ShapeDtypeStruct((rows, width...  54.7 us
    unnamed x1, local copies, waits for them, and re-layouts  1.62 us

profile of v3, /device:TPU:0, one launch (start us, length us, event | category | flops | bytes accessed | tf_op | source)
XLA Modules:
  0.0 56.4 jit_solution(11609944174341424762)
XLA Ops:
  0.0 54.7 %shard_map.82 = bf16[128,768]{1,0:T(8,128)(2,1)} custom-call(bf16[128,768]{1,0:T(8,128)(2,1)} %q_ref.1, bf16[128,768]{1,0:T(8,128)(2,1)} %k_hbm.1, bf16[128,768]{1,0:T(8,128)(2,1)} %v_hbm.1, bf16[64,4096]{1,0:T(8,128)(2,1)} %cap_ref.1, bf16[4096,768]{1,0:T(8,128)(2,1)} %wk_hbm.1, bf16[4096,768]{1,0:T(8,128)(2,1)} %wv_hbm.1, s32[2,8]{1,0:T(2,128)} %bitcast.1, ...), custom_call_target="tpu_custom_call" | custom-call | tf_op jit(solution)/shard_map/pallas_call | solution.py:573
  54.8 1.6 %copy.10 = bf16[128,768]{1,0:T(8,128)(2,1)} copy(bf16[128,768]{1,0:T(8,128)(2,1)} %shard_map.82) | data formatting | bytes 393216

commit v4 on v3

--- a/solution.py
+++ b/solution.py
@@ -166,21 +166,18 @@
             device_id=sibling, device_id_type=MESH,
         )
 
-    def q_copy(source, slot, send, device):
+    half_rows = rows // 2
+
+    def q_copy(source, slot, u, send, b, device):
+        at = pl.ds(u * half_rows, half_rows)
         return pltpu.make_async_remote_copy(
-            source, q_all.at[slot], send, q_recv.at[slot], device_id=device, device_id_type=MESH
-        )
-
-    half_rows = rows // 2
+            source.at[at], q_all.at[slot, at], send.at[b, u], q_recv.at[slot, u],
+            device_id=device, device_id_type=MESH,
+        )
+
     odd = lax.rem(z, 2)
     partner_z = z + 1 - 2 * odd
     partner = (tm + 2 - 4 * odd, head)
-
-    def q_x_half(slot, b):
-        lower = q_all.at[slot, pl.ds(0, half_rows)]
-        return pltpu.make_async_remote_copy(
-            lower, lower, q_x_send.at[b], q_recv.at[slot], device_id=across_x, device_id_type=MESH
-        )
 
     def q_round(slot):
         upper = q_all.at[slot, pl.ds(half_rows, half_rows)]
@@ -217,15 +214,17 @@
     for j in range(CHUNKS):
         cap_to_y(j).start()
 
-    @pl.when(z < ZL - 1)
-    def _():
-        q_copy(q_ref, tm, q_up_send.at[z], above).start()
-
-    @pl.when(z > 0)
-    def _():
-        q_copy(q_ref, tm, q_down_send.at[z], below).start()
-
-    q_copy(q_ref, tm, q_x_send.at[z], across_x).start()
+    for u in range(2):
+
+        @pl.when(z < ZL - 1)
+        def _():
+            q_copy(q_ref, tm, u, q_up_send, z, above).start()
+
+        @pl.when(z > 0)
+        def _():
+            q_copy(q_ref, tm, u, q_down_send, z, below).start()
+
+        q_copy(q_ref, tm, u, q_x_send, z, across_x).start()
     for j in range(CHUNKS):
         cap_to_sibling(j).start()
 
@@ -242,50 +241,38 @@
         at = slice(h * HD, (h + 1) * HD)
         v_t[at, :rows] = v_ref[:, at].astype(jnp.float32).T.astype(jnp.bfloat16)
 
+    def q_on(k, u, b, send, onward, more):
+        came = x + 2 * b
+        arrived = q_copy(q_all.at[came], came, u, send, b, onward)
+        arrived.wait_recv()
+
+        @pl.when(more)
+        def _():
+            arrived.start()
+
+        over = q_copy(q_all.at[came], came, u, q_x_send, b, across_x)
+        if u == 1 and k == 1:
+            @pl.when(b != partner_z)
+            def _():
+                over.start()
+        else:
+            over.start()
+
     def q_step(k):
-        @pl.when(z >= k)
-        def _():
-            came = tm - 2 * k
-            q_copy(q_all.at[came], came, q_up_send.at[z - k], above).wait_recv()
-
-            @pl.when(z < ZL - 1)
-            def _():
-                q_copy(q_all.at[came], came, q_up_send.at[z - k], above).start()
-
-            if k == 1:
-                @pl.when(odd == 1)
-                def _():
-                    q_x_half(came, z - k).start()
-
-                @pl.when(jnp.logical_not(odd == 1))
-                def _():
-                    q_copy(q_all.at[came], came, q_x_send.at[z - k], across_x).start()
-            else:
-                q_copy(q_all.at[came], came, q_x_send.at[z - k], across_x).start()
-
-        @pl.when(z + k < ZL)
-        def _():
-            came = tm + 2 * k
-            q_copy(q_all.at[came], came, q_down_send.at[z + k], below).wait_recv()
-
-            @pl.when(z > 0)
-            def _():
-                q_copy(q_all.at[came], came, q_down_send.at[z + k], below).start()
-
-            if k == 1:
-                @pl.when(odd == 0)
-                def _():
-                    q_x_half(came, z + k).start()
-
-                @pl.when(jnp.logical_not(odd == 0))
-                def _():
-                    q_copy(q_all.at[came], came, q_x_send.at[z + k], across_x).start()
-            else:
-                q_copy(q_all.at[came], came, q_x_send.at[z + k], across_x).start()
+        for u in range(2):
+
+            @pl.when(z >= k)
+            def _():
+                q_on(k, u, z - k, q_up_send, above, z < ZL - 1)
+
+            @pl.when(z + k < ZL)
+            def _():
+                q_on(k, u, z + k, q_down_send, below, z > 0)
 
         if k == 1:
             beside = tm + 1 - 2 * x
-            q_copy(q_all.at[beside], beside, q_x_send.at[z], across_x).wait_recv()
+            for u in range(2):
+                q_copy(q_all.at[beside], beside, u, q_x_send, z, across_x).wait_recv()
             q_round(beside).start()
 
     tile = 256
@@ -315,13 +302,13 @@
     hand_on(0)
     q_step(1)
     hand_on(1)
+    hand_on(2)
+    q_step(2)
     project(0)
-    hand_on(2)
+    hand_on(3)
     project(1)
-    q_step(2)
-    hand_on(3)
+    q_step(3)
     project(2)
-    q_step(3)
     project(3)
 
     tk[...] = acc[:, :width].astype(jnp.bfloat16)
@@ -361,12 +348,13 @@
 
         @pl.when(to == partner_z)
         def _():
-            q_x_half(came, 0).wait_recv()
+            q_copy(q_all.at[came], came, 0, q_x_send, 0, across_x).wait_recv()
             q_round(came).wait_recv()
 
         @pl.when((to != partner_z) & (to != z))
         def _():
-            q_copy(q_all.at[came], came, q_x_send.at[0], across_x).wait_recv()
+            for u in range(2):
+                q_copy(q_all.at[came], came, u, q_x_send, 0, across_x).wait_recv()
 
         token = to * 2 * rows + lax.broadcasted_iota(jnp.int32, (8, 2 * rows), 1)
         token_shot = jnp.zeros((8, 2 * rows), jnp.int32)
@@ -524,21 +512,21 @@
     for b in range(ZL):
         slot_b = x + 2 * b
 
-        @pl.when((b <= z) & (z < ZL - 1))
-        def _():
-            q_copy(q_all.at[slot_b], slot_b, q_up_send.at[b], above).wait_send()
-
-        @pl.when((b >= z) & (z > 0))
-        def _():
-            q_copy(q_all.at[slot_b], slot_b, q_down_send.at[b], below).wait_send()
-
-        @pl.when(b == partner_z)
-        def _():
-            q_x_half(slot_b, b).wait_send()
+        for u in range(2):
+
+            @pl.when((b <= z) & (z < ZL - 1))
+            def _():
+                q_copy(q_all.at[slot_b], slot_b, u, q_up_send, b, above).wait_send()
+
+            @pl.when((b >= z) & (z > 0))
+            def _():
+                q_copy(q_all.at[slot_b], slot_b, u, q_down_send, b, below).wait_send()
+
+        q_copy(q_all.at[slot_b], slot_b, 0, q_x_send, b, across_x).wait_send()
 
         @pl.when(b != partner_z)
         def _():
-            q_copy(q_all.at[slot_b], slot_b, q_x_send.at[b], across_x).wait_send()
+            q_copy(q_all.at[slot_b], slot_b, 1, q_x_send, b, across_x).wait_send()
 
         for g in range(GROUPS):
             for copy in x_copies(b, g):
@@ -593,8 +581,8 @@
             dma((CHUNKS + 3,)),
         ]
         + [dma((CHUNKS,))] * 6
-        + [dma((2 * ZL,))]
-        + [dma((ZL,))] * 3
+        + [dma((2 * ZL, 2))]
+        + [dma((ZL, 2))] * 3
         + [dma((1,))] * 2
         + [dma((ZL, GROUPS))] * 10,
         compiler_params=pltpu.CompilerParams(

time: 56.5 us -> 55.4 us (0.981)
  Pallas kernels: 54.7 us -> 53.7 us
    pallas_call x1, Pallas kernels: 54.7 us -> 53.7 us  [merged_form(): pl.pallas_call(merged_kernel, out_shape=jax.ShapeDtypeStruct((rows, width...]
where the time goes in v4:
time: 55.4 us; the launch traced here: 55.3 us
  Pallas kernels  53.7 us (97%)
  local copies, waits for them, and re-layouts  1.62 us (3%)
    pallas_call x1, Pallas kernels, merged_form(): pl.pallas_call(merged_kernel, out_shape=jax.ShapeDtypeStruct((rows, width...  53.7 us
    unnamed x1, local copies, waits for them, and re-layouts  1.62 us

profile of v4, /device:TPU:0, one launch (start us, length us, event | category | flops | bytes accessed | tf_op | source)
XLA Modules:
  0.0 55.3 jit_solution(13288505379207802778)
XLA Ops:
  0.0 53.7 %shard_map.82 = bf16[128,768]{1,0:T(8,128)(2,1)} custom-call(bf16[128,768]{1,0:T(8,128)(2,1)} %q_ref.1, bf16[128,768]{1,0:T(8,128)(2,1)} %k_hbm.1, bf16[128,768]{1,0:T(8,128)(2,1)} %v_hbm.1, bf16[64,4096]{1,0:T(8,128)(2,1)} %cap_ref.1, bf16[4096,768]{1,0:T(8,128)(2,1)} %wk_hbm.1, bf16[4096,768]{1,0:T(8,128)(2,1)} %wv_hbm.1, s32[2,8]{1,0:T(2,128)} %bitcast.1, ...), custom_call_target="tpu_custom_call" | custom-call | tf_op jit(solution)/shard_map/pallas_call | solution.py:561
  53.7 1.6 %copy.10 = bf16[128,768]{1,0:T(8,128)(2,1)} copy(bf16[128,768]{1,0:T(8,128)(2,1)} %shard_map.82) | data formatting | bytes 393216

commit v5 on v4

--- a/solution.py
+++ b/solution.py
@@ -341,8 +341,7 @@
             ),
         )
 
-    @pl.loop(0, ZL)
-    def _(step):
+    def attend(step):
         to = line_order(z, step)
         came = other_column + 2 * to
 
@@ -498,11 +497,19 @@
             def _():
                 merge(to, g, [own, over_x, from_below, from_above], last=True)
 
-    @pl.loop(0, ZL)
-    def _(step):
-        to = line_order(z, step)
-        for g in range(GROUPS):
-            merge_step(to, g)
+    @pl.loop(0, ZL + 1)
+    def _(turn):
+        @pl.when(turn != 2)
+        def _():
+            attend(jnp.where(turn < 2, turn, turn - 1))
+
+        @pl.when((turn == 2) | (turn == ZL))
+        def _():
+            @pl.loop(jnp.where(turn == 2, 0, 1), jnp.where(turn == 2, 1, ZL))
+            def _(step):
+                to = line_order(z, step)
+                for g in range(GROUPS):
+                    merge_step(to, g)
 
     for j in range(CHUNKS):
         cap_to_y(j).wait_send()

time: 55.4 us -> 52.5 us (0.948)
  Pallas kernels: 53.7 us -> 50.7 us
    pallas_call x1, Pallas kernels: 53.7 us -> 50.7 us  [merged_form(): pl.pallas_call(merged_kernel, out_shape=jax.ShapeDtypeStruct((rows, width...]
where the time goes in v5:
time: 52.5 us; the launch traced here: 52.4 us
  Pallas kernels  50.7 us (97%)
  local copies, waits for them, and re-layouts  1.62 us (3%)
    pallas_call x1, Pallas kernels, merged_form(): pl.pallas_call(merged_kernel, out_shape=jax.ShapeDtypeStruct((rows, width...  50.7 us
    unnamed x1, local copies, waits for them, and re-layouts  1.62 us

profile of v5, /device:TPU:0, one launch (start us, length us, event | category | flops | bytes accessed | tf_op | source)
XLA Modules:
  0.0 52.4 jit_solution(16248030052588630782)
XLA Ops:
  0.0 50.7 %shard_map.82 = bf16[128,768]{1,0:T(8,128)(2,1)} custom-call(bf16[128,768]{1,0:T(8,128)(2,1)} %q_ref.1, bf16[128,768]{1,0:T(8,128)(2,1)} %k_hbm.1, bf16[128,768]{1,0:T(8,128)(2,1)} %v_hbm.1, bf16[64,4096]{1,0:T(8,128)(2,1)} %cap_ref.1, bf16[4096,768]{1,0:T(8,128)(2,1)} %wk_hbm.1, bf16[4096,768]{1,0:T(8,128)(2,1)} %wv_hbm.1, s32[2,8]{1,0:T(2,128)} %bitcast.1, ...), custom_call_target="tpu_custom_call" | custom-call | tf_op jit(solution)/shard_map/pallas_call | solution.py:568
  50.7 1.6 %copy.10 = bf16[128,768]{1,0:T(8,128)(2,1)} copy(bf16[128,768]{1,0:T(8,128)(2,1)} %shard_map.82) | data formatting | bytes 393216
